TPU v7x, 512 devices: a whole 4x8x8 slice. The times are simulated.
512 devices in a mesh: seq: 32 (over y, z_hi, core), chan: 16 (over x, z_lo).
Axes of the slice: x: 4, y: 8, z: 8 (z_hi: 2, z_lo: 4; z = z_hi * 4 + z_lo), core: 2. Of those that a mesh axis runs over, the one named last changes fastest.
Arguments:
- projected: bfloat16 [16384, 3, 4096], P('seq', None, 'chan'), may hold values from -6 to 6
- short_w: float32 [3, 3, 4096], P(None, None, 'chan'), may hold values from -3.5 to 3.5
- residues: float32 [4096, 16], P('chan'), may hold values from -1.5 to 1.5
- rates: float32 [4096, 16], P('chan'), may hold values from 0.5 to 500
- skip: float32 [4096], P('chan'), may hold values from 0.5 to 1.5
- w_out: bfloat16 [4096, 8192], P('seq', 'chan'), may hold values from -0.09375 to 0.09375
Outputs:
- layer_out: bfloat16 [16384, 8192], P('seq', 'chan')
All inputs are finite; a program needn't handle non-finite values.
Results may differ from a plain program's by a relative error of at most 0.015.
Values may be sent and summed in bfloat16 or wider, within the bound.
A program may use at most 64 MiB of HBM per device.

v0:
```python
import functools

import jax
import jax.numpy as jnp
from jax import lax
from jax.experimental import pallas as pl
from jax.experimental.pallas import tpu as pltpu
from jax.sharding import PartitionSpec as P

MESH = pl.DeviceIdType.MESH
MODES = 16
SUBS = 8
LANES = 128
F32, BF16 = jnp.float32, jnp.bfloat16


def rounded(value):
    return value.astype(BF16).astype(F32)


def total_of(terms):
    terms = list(terms)
    while len(terms) > 1:
        terms = [a + b for a, b in zip(terms[::2], terms[1::2])] + terms[len(terms) // 2 * 2 :]
    return terms[0]


def kernel(
    length,
    proj,
    short_w,
    res,
    rate,
    skip,
    w_own,
    out,
    wide,
    coef,
    dec,
    sub_dec,
    u_buf,
    q_buf,
    y_buf,
    part,
    own_total,
    pair,
    msg,
    g_wide,
    g_all,
    w_all,
    acc,
    pair_sem,
    msg_send,
    msg_recv,
    w_send,
    w_recv,
    z_send,
    z_recv,
    x_send,
    x_recv,
):
    s = lax.axis_index("seq")
    c = lax.axis_index("chan")
    y, zh, k = s // 4, (s // 2) % 2, s % 2
    x, zl = c // 4, c % 4
    h = s // 2
    tokens, chans = proj.shape[1], proj.shape[2]
    tiles = chans // LANES
    steps = tokens // SUBS
    half = tokens // 2

    def seq_of(yy, zz, kk):
        return yy * 4 + zz * 2 + kk

    up_y, down_y = (y + 1) % 8, (y + 7) % 8
    right, left, across = (x + 1) % 4, (x + 3) % 4, (x + 2) % 4
    partner = seq_of(y, zh, 1 - k)

    barrier = pltpu.get_barrier_semaphore()

    def greet(seq, chan):
        pl.semaphore_signal(barrier, inc=1, device_id=(seq, chan), device_id_type=MESH)

    greet(partner, c)
    for step in (1, 3):
        greet(s, (x + step) % 4 * 4 + zl)
        greet(s, x * 4 + (zl + step) % 4)

    def greet_chip(step, _):
        greet((h + step) % 16 * 2 + k, c)
        return 0

    lax.fori_loop(1, 16, greet_chip, 0)

    speed = rate[...] * (1.0 / length)
    scale = res[...] * jnp.sqrt(2.0 * rate[...] * (1.0 / length))
    coef[...] = scale

    def decay(count):
        return jnp.exp(speed * (-1.0 * count))

    for at, count in enumerate((1, steps, 2 * steps, 4 * steps)):
        dec[at] = decay(count)
    sub = lax.broadcasted_iota(jnp.int32, (SUBS, chans), 0)
    sub_steps = sub.astype(F32) * (-1.0 * steps)
    for m in range(MODES):
        sub_dec[m] = jnp.exp(jnp.broadcast_to(speed[m : m + 1], (SUBS, chans)) * sub_steps)

    for stream in range(3):
        for tile in range(tiles):
            lanes = pl.ds(tile * LANES, LANES)
            wide[stream, tile, 0:8, :] = jnp.zeros((8, LANES), F32)
            wide[stream, tile, 8 : 8 + tokens, :] = proj[stream, :, lanes].astype(F32)

    sub1 = lax.broadcasted_iota(jnp.int32, (SUBS, LANES), 0)
    keep = jnp.where((sub1 > 0) | (s == 0), 1.0, 0.0).astype(F32)

    def row(ref, lanes, *index):
        return jnp.broadcast_to(ref[index + (lanes,)], (SUBS, LANES))

    for tile in range(tiles):
        lanes = pl.ds(tile * LANES, LANES)
        taps = [[row(short_w, lanes, j, slice(st, st + 1)) for j in range(3)] for st in range(3)]
        skip_row = row(skip, lanes, slice(0, 1))

        def rows_at(stream, start, tile=tile):
            return wide[stream, tile, pl.ds(start, SUBS, stride=steps), :]

        def scan_step(i, carry, first=False, tile=tile, lanes=lanes, taps=taps, skip_row=skip_row):
            state, behind = carry
            feats, now = [], []
            for st in range(3):
                value = rows_at(st, 8 + i)
                one, two = behind[st]
                feats.append(taps[st][0] * value + taps[st][1] * one + taps[st][2] * two)
                now.append((value, one))
            u = rounded(feats[1] * feats[2])
            if first:
                u = u * keep
            state = tuple(
                row(dec, lanes, 0, slice(m, m + 1)) * state[m] + row(coef, lanes, slice(m, m + 1)) * u
                for m in range(MODES)
            )
            q_buf[i, :, lanes] = rounded(feats[0])
            u_buf[i, :, lanes] = u
            y_buf[i, :, lanes] = total_of(state) + skip_row * u
            return state, tuple(now)

        carry = (
            tuple(jnp.zeros((SUBS, LANES), F32) for _ in range(MODES)),
            tuple((rows_at(st, 7), rows_at(st, 6)) for st in range(3)),
        )
        carry = scan_step(0, carry, True)
        carry = scan_step(1, carry, True)
        state, _ = lax.fori_loop(2, steps, scan_step, carry)
        for m in range(MODES):
            value = state[m]
            for at, shift in ((1, 1), (2, 2), (3, 4)):
                moved = pltpu.roll(value, shift, 0)
                value = value + row(dec, lanes, at, slice(m, m + 1)) * jnp.where(sub1 >= shift, moved, 0.0)
            own_total[m : m + 1, lanes] = value[SUBS - 1 : SUBS]
            part[m, :, lanes] = jnp.where(sub1 >= 1, pltpu.roll(value, 1, 0), 0.0)

    def ends(stream, first):
        start = 0 if first else tokens - 2
        return jnp.concatenate([wide[stream, t, pl.ds(8 + start, 2), :] for t in range(tiles)], axis=1)

    mine = [own_total[...]]
    mine += [ends(1, True), ends(2, True), ends(1, False), ends(2, False), ends(0, False)]
    mine += [jnp.zeros((6, chans), F32)]
    pair[0] = jnp.concatenate(mine, axis=0).astype(BF16)

    pl.semaphore_wait(barrier, 20)

    pair_copy = pltpu.make_async_remote_copy(
        src_ref=pair.at[0], dst_ref=pair.at[1], send_sem=pair_sem.at[0], recv_sem=pair_sem.at[1],
        device_id=(partner, c), device_id_type=MESH,
    )
    pair_copy.start()

    def w_copy(slot, at, seq):
        return pltpu.make_async_remote_copy(
            src_ref=w_all.at[slot], dst_ref=w_all.at[slot], send_sem=w_send.at[at], recv_sem=w_recv.at[slot],
            device_id=(seq, c), device_id_type=MESH,
        )

    w_started = []

    def w_go(slot, seq):
        copy = w_copy(slot, len(w_started), seq)
        copy.start()
        w_started.append(copy)

    def w_here(slot):
        w_copy(slot, 0, partner).wait_recv()

    w_all[s] = w_own[...]
    pair_copy.wait()

    def short(stream, two, one, zero):
        w0, w1, w2 = (short_w[j, stream : stream + 1, :] for j in range(3))
        return w0 * zero + w1 * one + w2 * two

    def edge(last, first, streams):
        gives = []
        for stream, before, own in zip(streams, last, first):
            gives.append(
                (
                    short(stream, before[0:1], before[1:2], own[0:1]),
                    short(stream, before[1:2], own[0:1], own[1:2]),
                )
            )
        return gives

    def edge_inner(last, first):
        (k0, k1), (v0, v1) = edge(last, first, (1, 2))
        return rounded(k0 * v0), rounded(k1 * v1)

    own_t, other_t = own_total[...], pair[1, 0:16, :].astype(F32)
    own_edges, other_edges = pair[0, 16:32, :].astype(F32), pair[1, 16:32, :].astype(F32)
    low = k == 0
    t_low, t_high = jnp.where(low, own_t, other_t), jnp.where(low, other_t, own_t)
    e_low, e_high = jnp.where(low, own_edges, other_edges), jnp.where(low, other_edges, own_edges)
    m0, m1 = edge_inner((e_low[4:6], e_low[6:8]), (e_high[0:2], e_high[2:4]))
    chip_total = decay(tokens) * t_low + t_high + scale * (decay(tokens - 1) * m0 + decay(tokens - 2) * m1)
    message = jnp.concatenate([chip_total, e_low[0:4], e_high[4:10], jnp.zeros((6, chans), F32)], axis=0)
    msg[h] = message.astype(BF16)

    def msg_copy(slot, step, chip):
        return pltpu.make_async_remote_copy(
            src_ref=msg.at[slot], dst_ref=msg.at[slot], send_sem=msg_send.at[step], recv_sem=msg_recv.at[slot],
            device_id=(chip * 2 + k, c), device_id_type=MESH,
        )

    def msg_go(step, _):
        msg_copy(h, step, h + step).start()
        return 0

    lax.fori_loop(1, 16 - h, msg_go, 0)

    other_z = 1 - zh
    w_go(s, seq_of(y, other_z, k))
    w_go(s, seq_of(up_y, zh, k))
    w_go(s, seq_of(down_y, zh, k))
    w_go(s, partner)

    far = decay(2 * tokens)
    far1, far2 = scale * decay(2 * tokens - 1), scale * decay(2 * tokens - 2)

    def add_chip(j, carry):
        state, last = carry
        msg_copy(j, 0, h).wait_recv()
        total, edges = msg[j, 0:16, :].astype(F32), msg[j, 16:32, :].astype(F32)
        u0, u1 = edge_inner((last[0:2], last[2:4]), (edges[0:2], edges[2:4]))
        after = jnp.where(j == 0, 0.0, 1.0)
        return far * state + total + after * (far1 * u0 + far2 * u1), edges[4:10]

    chip_in, last = lax.fori_loop(0, h, add_chip, (jnp.zeros((MODES, chans), F32), jnp.zeros((6, chans), F32)))
    f0, f1 = edge_inner((last[0:2], last[2:4]), (e_low[0:2], e_low[2:4]))
    chip_first = jnp.where(h == 0, 0.0, 1.0)
    high_in = decay(tokens) * chip_in + t_low
    high_in += chip_first * scale * (decay(tokens - 1) * f0 + decay(tokens - 2) * f1)
    state_in = jnp.where(low, chip_in, high_in)
    u_first = (jnp.where(low, f0 * chip_first, m0), jnp.where(low, f1 * chip_first, m1))
    first_in = scale * (decay(steps - 1) * u_first[0] + decay(steps - 2) * u_first[1])
    q_last = jnp.where(low, last[4:6], e_low[8:10])
    q_first = edge((q_last,), (ends(0, True),), (0,))[0]

    for tile in range(tiles):
        cut = slice(tile * LANES, tile * LANES + LANES)
        lanes = pl.ds(tile * LANES, LANES)
        skip_row = row(skip, lanes, slice(0, 1))
        state = []
        for m in range(MODES):
            fade = sub_dec[m, :, lanes]
            after = jnp.where(sub1 >= 1, pltpu.roll(fade, 1, 0), 0.0)
            state.append(
                part[m, :, lanes]
                + fade * jnp.broadcast_to(state_in[m : m + 1, cut], (SUBS, LANES))
                + after * jnp.broadcast_to(first_in[m : m + 1, cut], (SUBS, LANES))
            )
        state = tuple(state)

        def gate_step(i, state, first=None, lanes=lanes, tile=tile, cut=cut, skip_row=skip_row):
            state = tuple(row(dec, lanes, 0, slice(m, m + 1)) * state[m] for m in range(MODES))
            conv, q = y_buf[i, :, lanes], q_buf[i, :, lanes]
            if first is not None:
                u = jnp.where(sub1 == 0, jnp.broadcast_to(u_first[first][:, cut], (SUBS, LANES)), 0.0)
                state = tuple(state[m] + row(coef, lanes, slice(m, m + 1)) * u for m in range(MODES))
                conv = conv + skip_row * u
                q = jnp.where(sub1 == 0, jnp.broadcast_to(rounded(q_first[first][:, cut]), (SUBS, LANES)), q)
            conv = rounded(conv + total_of(state))
            g_wide[tile, pl.ds(i, SUBS, stride=steps), :] = q * conv
            return state

        state = gate_step(0, state, 0)
        state = gate_step(1, state, 1)
        lax.fori_loop(2, steps, gate_step, state)
    for tile in range(tiles):
        g_all[c, :, pl.ds(tile * LANES, LANES)] = g_wide[tile].astype(BF16)

    end = (zl == 0) | (zl == 3)
    beside = x * 4 + zl + 1 - 2 * (zl % 2)
    middle = x * 4 + 3 - zl
    order = (zl, zl + 1 - 2 * (zl % 2), 2 - zl // 2, 3 - 3 * (zl // 2))

    def z_copy(slot, at, chan):
        return pltpu.make_async_remote_copy(
            src_ref=g_all.at[slot], dst_ref=g_all.at[slot], send_sem=z_send.at[at], recv_sem=z_recv.at[slot % 4],
            device_id=(s, chan), device_id_type=MESH,
        )

    def x_copy(slot, piece, at, xx):
        rows = pl.ds(piece * half, half)
        return pltpu.make_async_remote_copy(
            src_ref=g_all.at[slot, rows], dst_ref=g_all.at[slot, rows], send_sem=x_send.at[at],
            recv_sem=x_recv.at[slot, piece], device_id=(s, xx * 4 + zl), device_id_type=MESH,
        )

    x_started = []

    def x_go(slot, piece, xx):
        copy = x_copy(slot, piece, len(x_started), xx)
        copy.start()
        x_started.append(copy)

    def own_go(i):
        slot = x * 4 + order[i]
        if i == 0:
            z_copy(slot, 0, beside).start()
            pl.when(jnp.logical_not(end))(lambda: z_copy(slot, 1, middle).start())
        else:
            z_copy(slot, 0, beside).wait_recv()
            onward = middle if i == 1 else beside
            pl.when(jnp.logical_not(end))(lambda: z_copy(slot, 1 + i, onward).start())
        x_go(slot, 0, right)
        x_go(slot, 1, left)
        x_go(slot, 1, right)
        x_go(slot, 0, left)

    def pass_on(i):
        slot = left * 4 + order[i]
        x_copy(slot, 0, 0, right).wait_recv()
        x_go(slot, 0, right)
        slot = right * 4 + order[i]
        x_copy(slot, 1, 0, right).wait_recv()
        x_go(slot, 1, left)

    def multiply(i):
        x_copy(left * 4 + order[i], 1, 0, right).wait_recv()
        x_copy(right * 4 + order[i], 0, 0, right).wait_recv()
        x_copy(across * 4 + order[i], 0, 0, right).wait_recv()
        x_copy(across * 4 + order[i], 1, 0, right).wait_recv()

        def block(xx, _):
            slot = xx * 4 + order[i]
            rows = w_all[pl.ds(2 * slot, 2)].reshape(chans, -1)
            for piece in range(2):
                at = pl.ds(piece * half, half)
                part_sum = jnp.dot(g_all[slot, at], rows, preferred_element_type=F32)
                acc[at] = acc[at] + part_sum
            return 0

        lax.fori_loop(0, 4, block, 0)

    def w_step(n):
        if n == 1:
            slot = seq_of(y, other_z, k)
            w_here(slot)
            w_go(slot, seq_of(up_y, zh, k))
            w_go(slot, seq_of(down_y, zh, k))
            w_go(slot, partner)
        for zz, ups, downs in ((zh, 4, 3), (other_z, 3, 4)):
            for here, limit, onward in (((y + 8 - n) % 8, ups, up_y), ((y + n) % 8, downs, down_y)):
                if n <= limit:
                    slot = seq_of(here, zz, k)
                    w_here(slot)
                    if n < limit:
                        w_go(slot, seq_of(onward, zh, k))
                    w_go(slot, partner)

    acc[...] = jnp.zeros_like(acc)
    own_go(0)
    w_step(1)
    own_go(1)
    pass_on(0)
    w_step(2)
    own_go(2)
    pass_on(1)
    w_step(3)
    own_go(3)
    pass_on(2)
    w_step(4)

    def w_other(at, _):
        w_here(at * 2 + 1 - k)
        return 0

    lax.fori_loop(0, 16, w_other, 0)
    multiply(0)
    multiply(1)
    pass_on(3)
    multiply(2)
    multiply(3)
    out[...] = acc[...].astype(BF16)

    for copy in x_started + w_started:
        copy.wait_send()
    z_copy(c, 0, beside).wait_send()

    @pl.when(jnp.logical_not(end))
    def _():
        for at in range(1, 5):
            z_copy(c, at, beside).wait_send()

    def msg_gone(step, _):
        msg_copy(h, step, h).wait_send()
        return 0

    lax.fori_loop(1, 16 - h, msg_gone, 0)


def body(projected, short_w, residues, rates, skip, w_out):
    tokens, _, chans = projected.shape
    rows, feats = w_out.shape
    length = tokens * lax.axis_size("seq")
    tiles, steps = chans // LANES, tokens // SUBS
    vmem = pl.BlockSpec(memory_space=pltpu.VMEM)
    dma = pltpu.SemaphoreType.DMA
    return pl.pallas_call(
        functools.partial(kernel, length),
        out_shape=jax.ShapeDtypeStruct((tokens, feats), BF16),
        in_specs=[vmem] * 6,
        out_specs=vmem,
        scratch_shapes=[
            pltpu.VMEM((3, tiles, 8 + tokens, LANES), F32),
            pltpu.VMEM((MODES, chans), F32),
            pltpu.VMEM((4, MODES, chans), F32),
            pltpu.VMEM((MODES, SUBS, chans), F32),
            pltpu.VMEM((steps, SUBS, chans), F32),
            pltpu.VMEM((steps, SUBS, chans), F32),
            pltpu.VMEM((steps, SUBS, chans), F32),
            pltpu.VMEM((MODES, SUBS, chans), F32),
            pltpu.VMEM((MODES, chans), F32),
            pltpu.VMEM((2, 32, chans), BF16),
            pltpu.VMEM((16, 32, chans), BF16),
            pltpu.VMEM((tiles, tokens, LANES), F32),
            pltpu.VMEM((16, tokens, chans), BF16),
            pltpu.VMEM((32, rows, feats), BF16),
            pltpu.VMEM((tokens, feats), F32),
            dma((2,)),
            dma((16,)),
            dma((16,)),
            dma((32,)),
            dma((32,)),
            dma((5,)),
            dma((4,)),
            dma((24,)),
            dma((16, 2)),
        ],
        compiler_params=pltpu.CompilerParams(
            collective_id=0, has_side_effects=True, vmem_limit_bytes=48 << 20
        ),
        cost_estimate=pl.CostEstimate(flops=2 * tokens * feats * 4096, bytes_accessed=4 << 20, transcendentals=0),
    )(projected.transpose(1, 0, 2), short_w, residues.T, rates.T, skip.reshape(1, chans), w_out)


def solution(mesh):
    return jax.shard_map(
        body,
        mesh=mesh,
        in_specs=(
            P("seq", None, "chan"),
            P(None, None, "chan"),
            P("chan", None),
            P("chan", None),
            P("chan"),
            P("seq", "chan"),
        ),
        out_specs=P("seq", "chan"),
        check_vma=False,
    )
```

profile of v0, /device:TPU:56, one launch (start us, length us, event | category | flops | bytes accessed | tf_op | source)
XLA Modules:
  0.0 73.9 jit_solution(11785943683358473555)
XLA Ops:
  0.0 0.0 copy-start.5
  0.0 0.7 copy-done.5
  0.7 0.0 copy-start
  0.7 1.1 %copy-done = bf16[512,3,256]{2,0,1:T(8,128)(2,1)S(1)} copy-done((bf16[512,3,256]{2,0,1:T(8,128)(2,1)S(1)}, bf16[512,3,256]{2,0,1:T(8,128)(2,1)}, u32[]{:S(2)}) %copy-start) | copy-done | bytes 786456
  1.8 0.0 copy-start.1
  1.8 0.9 %copy-done.1 = bf16[128,512]{1,0:T(8,128)(2,1)S(1)} copy-done((bf16[128,512]{1,0:T(8,128)(2,1)S(1)}, bf16[128,512]{1,0:T(8,128)(2,1)}, u32[]{:S(2)}) %copy-start.1) | copy-done | bytes 131096
  2.7 0.0 copy-start.2
  2.7 0.7 copy-done.2
  3.4 0.0 copy-start.3
  3.4 0.7 copy-done.3
  4.2 0.0 copy-start.4
  4.2 0.7 copy-done.4
  4.9 68.2 %shard_map.64 = bf16[512,512]{1,0:T(8,128)(2,1)S(1)} custom-call(bf16[3,512,256]{2,1,0:T(8,128)(2,1)S(1)} %bitcast.4, f32[3,3,256]{2,1,0:T(4,128)S(1)} %copy-done.4, f32[16,256]{1,0:T(8,128)S(1)} %bitcast.5, f32[16,256]{1,0:T(8,128)S(1)} %bitcast.6, f32[1,256]{1,0:T(1,128)S(1)} %bitcast.7, bf16[128,512]{1,0:T(8,128)(2,1)S(1)} %copy-done.1), custom_call_target="tpu_custom_call" | custom-call | flops 2147483648 | bytes 4194304 | tf_op jit(solution)/shard_map/pallas_call | solution.py:430
  73.1 0.8 %copy.8 = bf16[512,512]{1,0:T(8,128)(2,1)} copy(bf16[512,512]{1,0:T(8,128)(2,1)S(1)} %shard_map.64) | data formatting | bytes 1048576
Async XLA Ops:
  0.0 0.7 copy-start.5
  0.7 1.1 %copy-start = (bf16[512,3,256]{2,0,1:T(8,128)(2,1)S(1)}, bf16[512,3,256]{2,0,1:T(8,128)(2,1)}, u32[]{:S(2)}) copy-start(bf16[512,3,256]{2,0,1:T(8,128)(2,1)} %param.6) | copy-start | bytes 2359300
  1.8 0.9 %copy-start.1 = (bf16[128,512]{1,0:T(8,128)(2,1)S(1)}, bf16[128,512]{1,0:T(8,128)(2,1)}, u32[]{:S(2)}) copy-start(bf16[128,512]{1,0:T(8,128)(2,1)} %w_own.1) | copy-start | bytes 393220
  2.7 0.7 copy-start.2
  3.4 0.7 copy-start.3
  4.2 0.7 copy-start.4
where the time goes:
time: 74.2 us; the launch traced here: 73.9 us
  Pallas kernels  68.2 us (92%)
  local copies, waits for them, and re-layouts  5.65 us (8%)
    pallas_call x1, Pallas kernels, body(): pl.pallas_call(functools.partial(kernel, length), out_shape=jax.ShapeDtyp...  68.2 us
    unnamed x13, local copies, waits for them, and re-layouts  5.65 us

commit v1 on v0

--- a/solution.py
+++ b/solution.py
@@ -11,6 +11,7 @@
 MODES = 16
 SUBS = 8
 LANES = 128
+PIECES = 4
 F32, BF16 = jnp.float32, jnp.bfloat16
 
 
@@ -27,13 +28,18 @@
 
 def kernel(
     length,
+    proj_hbm,
+    short_hbm,
+    res_hbm,
+    rate_hbm,
+    skip_hbm,
+    w_hbm,
+    out,
     proj,
     short_w,
     res,
     rate,
     skip,
-    w_own,
-    out,
     wide,
     coef,
     dec,
@@ -45,10 +51,13 @@
     own_total,
     pair,
     msg,
+    edges,
+    firsts,
     g_wide,
     g_all,
     w_all,
     acc,
+    load_sem,
     pair_sem,
     msg_send,
     msg_recv,
@@ -67,7 +76,7 @@
     tokens, chans = proj.shape[1], proj.shape[2]
     tiles = chans // LANES
     steps = tokens // SUBS
-    half = tokens // 2
+    rows_of_piece = tokens // PIECES
 
     def seq_of(yy, zz, kk):
         return yy * 4 + zz * 2 + kk
@@ -75,6 +84,13 @@
     up_y, down_y = (y + 1) % 8, (y + 7) % 8
     right, left, across = (x + 1) % 4, (x + 3) % 4, (x + 2) % 4
     partner = seq_of(y, zh, 1 - k)
+
+    loads = []
+    for at, (source, target) in enumerate(
+        ((rate_hbm, rate), (res_hbm, res), (short_hbm, short_w), (skip_hbm, skip), (proj_hbm, proj), (w_hbm, w_all.at[s]))
+    ):
+        loads.append(pltpu.make_async_copy(source, target, load_sem.at[at]))
+        loads[-1].start()
 
     barrier = pltpu.get_barrier_semaphore()
 
@@ -92,6 +108,11 @@
 
     lax.fori_loop(1, 16, greet_chip, 0)
 
+    acc[...] = jnp.zeros_like(acc)
+    edges[...] = jnp.zeros_like(edges)
+
+    for copy in loads[:4]:
+        copy.wait()
     speed = rate[...] * (1.0 / length)
     scale = res[...] * jnp.sqrt(2.0 * rate[...] * (1.0 / length))
     coef[...] = scale
@@ -106,6 +127,7 @@
     for m in range(MODES):
         sub_dec[m] = jnp.exp(jnp.broadcast_to(speed[m : m + 1], (SUBS, chans)) * sub_steps)
 
+    loads[4].wait()
     for stream in range(3):
         for tile in range(tiles):
             lanes = pl.ds(tile * LANES, LANES)
@@ -194,7 +216,6 @@
     def w_here(slot):
         w_copy(slot, 0, partner).wait_recv()
 
-    w_all[s] = w_own[...]
     pair_copy.wait()
 
     def short(stream, two, one, zero):
@@ -238,6 +259,7 @@
 
     lax.fori_loop(1, 16 - h, msg_go, 0)
 
+    loads[5].wait()
     other_z = 1 - zh
     w_go(s, seq_of(y, other_z, k))
     w_go(s, seq_of(up_y, zh, k))
@@ -247,23 +269,52 @@
     far = decay(2 * tokens)
     far1, far2 = scale * decay(2 * tokens - 1), scale * decay(2 * tokens - 2)
 
-    def add_chip(j, carry):
-        state, last = carry
+    def put_edges(j):
+        values = msg[j, 16:32, :].astype(F32)
+        for tile in range(tiles):
+            edges[tile, pl.ds(j * 16 + 16, 16), :] = values[:, tile * LANES : tile * LANES + LANES]
+
+    def chip_here(j, _):
         msg_copy(j, 0, h).wait_recv()
-        total, edges = msg[j, 0:16, :].astype(F32), msg[j, 16:32, :].astype(F32)
-        u0, u1 = edge_inner((last[0:2], last[2:4]), (edges[0:2], edges[2:4]))
+        put_edges(j)
+        return 0
+
+    put_edges(h)
+    lax.fori_loop(0, h, chip_here, 0)
+    for tile in range(tiles):
+        lanes = pl.ds(tile * LANES, LANES)
+
+        def taps_of(stream, lanes=lanes):
+            return [jnp.broadcast_to(short_w[j, stream : stream + 1, lanes], (16, LANES)) for j in range(3)]
+
+        def edge_rows(at, before, tile=tile):
+            return edges[tile, pl.ds(at + (0 if before else 16), 16, stride=16), :]
+
+        (k0, k1), (v0, v1) = (
+            (
+                w0 * edge_rows(2 * st, False) + w1 * edge_rows(5 + 2 * st, True) + w2 * edge_rows(4 + 2 * st, True),
+                w0 * edge_rows(2 * st + 1, False) + w1 * edge_rows(2 * st, False) + w2 * edge_rows(5 + 2 * st, True),
+            )
+            for st, (w0, w1, w2) in enumerate((taps_of(1), taps_of(2)))
+        )
+        firsts[0, :, lanes] = rounded(k0 * v0)
+        firsts[1, :, lanes] = rounded(k1 * v1)
+
+    def add_chip(j, state):
         after = jnp.where(j == 0, 0.0, 1.0)
-        return far * state + total + after * (far1 * u0 + far2 * u1), edges[4:10]
-
-    chip_in, last = lax.fori_loop(0, h, add_chip, (jnp.zeros((MODES, chans), F32), jnp.zeros((6, chans), F32)))
-    f0, f1 = edge_inner((last[0:2], last[2:4]), (e_low[0:2], e_low[2:4]))
+        u0, u1 = firsts[0, pl.ds(j, 1), :], firsts[1, pl.ds(j, 1), :]
+        return far * state + msg[j, 0:16, :].astype(F32) + after * (far1 * u0 + far2 * u1)
+
+    chip_in = lax.fori_loop(0, h, add_chip, jnp.zeros((MODES, chans), F32))
+    f0, f1 = firsts[0, pl.ds(h, 1), :], firsts[1, pl.ds(h, 1), :]
     chip_first = jnp.where(h == 0, 0.0, 1.0)
+    chip_last_q = jnp.concatenate([edges[tile, pl.ds(h * 16 + 8, 2), :] for tile in range(tiles)], axis=1)
     high_in = decay(tokens) * chip_in + t_low
     high_in += chip_first * scale * (decay(tokens - 1) * f0 + decay(tokens - 2) * f1)
     state_in = jnp.where(low, chip_in, high_in)
     u_first = (jnp.where(low, f0 * chip_first, m0), jnp.where(low, f1 * chip_first, m1))
     first_in = scale * (decay(steps - 1) * u_first[0] + decay(steps - 2) * u_first[1])
-    q_last = jnp.where(low, last[4:6], e_low[8:10])
+    q_last = jnp.where(low, chip_last_q, e_low[8:10])
     q_first = edge((q_last,), (ends(0, True),), (0,))[0]
 
     for tile in range(tiles):
@@ -304,14 +355,15 @@
     middle = x * 4 + 3 - zl
     order = (zl, zl + 1 - 2 * (zl % 2), 2 - zl // 2, 3 - 3 * (zl // 2))
 
-    def z_copy(slot, at, chan):
+    def z_copy(slot, piece, at, chan):
+        rows = pl.ds(piece * rows_of_piece, rows_of_piece)
         return pltpu.make_async_remote_copy(
-            src_ref=g_all.at[slot], dst_ref=g_all.at[slot], send_sem=z_send.at[at], recv_sem=z_recv.at[slot % 4],
-            device_id=(s, chan), device_id_type=MESH,
+            src_ref=g_all.at[slot, rows], dst_ref=g_all.at[slot, rows], send_sem=z_send.at[at, piece],
+            recv_sem=z_recv.at[slot % 4, piece], device_id=(s, chan), device_id_type=MESH,
         )
 
     def x_copy(slot, piece, at, xx):
-        rows = pl.ds(piece * half, half)
+        rows = pl.ds(piece * rows_of_piece, rows_of_piece)
         return pltpu.make_async_remote_copy(
             src_ref=g_all.at[slot, rows], dst_ref=g_all.at[slot, rows], send_sem=x_send.at[at],
             recv_sem=x_recv.at[slot, piece], device_id=(s, xx * 4 + zl), device_id_type=MESH,
@@ -324,44 +376,54 @@
         copy.start()
         x_started.append(copy)
 
-    def own_go(i):
+    def x_here(slot, piece):
+        x_copy(slot, piece, 0, right).wait_recv()
+
+    def own_go():
+        for piece in range(PIECES):
+            z_copy(c, piece, 0, beside).start()
+            x_go(c, piece, right)
+            pl.when(jnp.logical_not(end))(lambda piece=piece: z_copy(c, piece, 1, middle).start())
+            x_go(c, (piece + PIECES // 2) % PIECES, left)
+
+    def along(i, piece):
         slot = x * 4 + order[i]
-        if i == 0:
-            z_copy(slot, 0, beside).start()
-            pl.when(jnp.logical_not(end))(lambda: z_copy(slot, 1, middle).start())
+        z_copy(slot, piece, 0, beside).wait_recv()
+        onward = middle if i == 1 else beside
+        pl.when(jnp.logical_not(end))(lambda: z_copy(slot, piece, 1 + i, onward).start())
+        x_go(slot, piece, right)
+        x_go(slot, piece, left)
+
+    def pass_on(i, piece):
+        if piece < PIECES // 2:
+            slot, onward = left * 4 + order[i], right
         else:
-            z_copy(slot, 0, beside).wait_recv()
-            onward = middle if i == 1 else beside
-            pl.when(jnp.logical_not(end))(lambda: z_copy(slot, 1 + i, onward).start())
-        x_go(slot, 0, right)
-        x_go(slot, 1, left)
-        x_go(slot, 1, right)
-        x_go(slot, 0, left)
-
-    def pass_on(i):
-        slot = left * 4 + order[i]
-        x_copy(slot, 0, 0, right).wait_recv()
-        x_go(slot, 0, right)
-        slot = right * 4 + order[i]
-        x_copy(slot, 1, 0, right).wait_recv()
-        x_go(slot, 1, left)
-
-    def multiply(i):
-        x_copy(left * 4 + order[i], 1, 0, right).wait_recv()
-        x_copy(right * 4 + order[i], 0, 0, right).wait_recv()
-        x_copy(across * 4 + order[i], 0, 0, right).wait_recv()
-        x_copy(across * 4 + order[i], 1, 0, right).wait_recv()
-
-        def block(xx, _):
-            slot = xx * 4 + order[i]
-            rows = w_all[pl.ds(2 * slot, 2)].reshape(chans, -1)
-            for piece in range(2):
-                at = pl.ds(piece * half, half)
-                part_sum = jnp.dot(g_all[slot, at], rows, preferred_element_type=F32)
-                acc[at] = acc[at] + part_sum
+            slot, onward = right * 4 + order[i], left
+        x_here(slot, piece)
+        x_go(slot, piece, onward)
+
+    place = dict(own=x, left=left, right=right, across=across)
+
+    def multiply(i, sides):
+        for piece in range(PIECES):
+            if 'left' in sides and piece >= PIECES // 2:
+                x_here(left * 4 + order[i], piece)
+            if 'right' in sides and piece < PIECES // 2:
+                x_here(right * 4 + order[i], piece)
+            if 'across' in sides:
+                x_here(across * 4 + order[i], piece)
+
+        def block(at, _):
+            at = pl.ds(pl.multiple_of(at * 256, 256), 256)
+            value = acc[at]
+            for side in sides:
+                slot = place[side] * 4 + order[i]
+                rows = w_all[pl.ds(2 * slot, 2)].reshape(chans, -1)
+                value = value + jnp.dot(g_all[slot, at], rows, preferred_element_type=F32)
+            acc[at] = value
             return 0
 
-        lax.fori_loop(0, 4, block, 0)
+        lax.fori_loop(0, tokens // 256, block, 0)
 
     def w_step(n):
         if n == 1:
@@ -379,39 +441,54 @@
                         w_go(slot, seq_of(onward, zh, k))
                     w_go(slot, partner)
 
-    acc[...] = jnp.zeros_like(acc)
-    own_go(0)
-    w_step(1)
-    own_go(1)
-    pass_on(0)
-    w_step(2)
-    own_go(2)
-    pass_on(1)
-    w_step(3)
-    own_go(3)
-    pass_on(2)
-    w_step(4)
-
     def w_other(at, _):
         w_here(at * 2 + 1 - k)
         return 0
 
+    own_go()
+    w_step(1)
+    along(1, 0)
+    along(1, 1)
+    pass_on(0, 0)
+    pass_on(0, 2)
+    along(2, 0)
+    pass_on(0, 1)
+    pass_on(0, 3)
+    along(1, 2)
+    along(2, 1)
+    along(1, 3)
+    along(2, 2)
+    along(2, 3)
+    w_step(2)
+    for piece in range(PIECES):
+        along(3, piece)
+    for piece in (0, 2, 1, 3):
+        pass_on(1, piece)
+    w_step(3)
+    for piece in (0, 2, 1, 3):
+        pass_on(2, piece)
+    w_step(4)
     lax.fori_loop(0, 16, w_other, 0)
-    multiply(0)
-    multiply(1)
-    pass_on(3)
-    multiply(2)
-    multiply(3)
+    everyone = tuple(place)
+    multiply(0, everyone)
+    multiply(1, everyone)
+    for piece in (0, 2, 1, 3):
+        pass_on(3, piece)
+    multiply(2, everyone)
+    multiply(3, ('own', 'left', 'right'))
+    multiply(3, ('across',))
     out[...] = acc[...].astype(BF16)
 
     for copy in x_started + w_started:
         copy.wait_send()
-    z_copy(c, 0, beside).wait_send()
+    for piece in range(PIECES):
+        z_copy(c, piece, 0, beside).wait_send()
 
     @pl.when(jnp.logical_not(end))
     def _():
         for at in range(1, 5):
-            z_copy(c, at, beside).wait_send()
+            for piece in range(PIECES):
+                z_copy(c, piece, at, beside).wait_send()
 
     def msg_gone(step, _):
         msg_copy(h, step, h).wait_send()
@@ -430,9 +507,14 @@
     return pl.pallas_call(
         functools.partial(kernel, length),
         out_shape=jax.ShapeDtypeStruct((tokens, feats), BF16),
-        in_specs=[vmem] * 6,
+        in_specs=[pl.BlockSpec(memory_space=pltpu.HBM)] * 6,
         out_specs=vmem,
         scratch_shapes=[
+            pltpu.VMEM((3, tokens, chans), BF16),
+            pltpu.VMEM((3, 3, chans), F32),
+            pltpu.VMEM((MODES, chans), F32),
+            pltpu.VMEM((MODES, chans), F32),
+            pltpu.VMEM((1, chans), F32),
             pltpu.VMEM((3, tiles, 8 + tokens, LANES), F32),
             pltpu.VMEM((MODES, chans), F32),
             pltpu.VMEM((4, MODES, chans), F32),
@@ -444,22 +526,25 @@
             pltpu.VMEM((MODES, chans), F32),
             pltpu.VMEM((2, 32, chans), BF16),
             pltpu.VMEM((16, 32, chans), BF16),
+            pltpu.VMEM((tiles, 17 * 16, LANES), F32),
+            pltpu.VMEM((2, 16, chans), F32),
             pltpu.VMEM((tiles, tokens, LANES), F32),
             pltpu.VMEM((16, tokens, chans), BF16),
             pltpu.VMEM((32, rows, feats), BF16),
             pltpu.VMEM((tokens, feats), F32),
+            dma((6,)),
             dma((2,)),
             dma((16,)),
             dma((16,)),
             dma((32,)),
             dma((32,)),
-            dma((5,)),
-            dma((4,)),
-            dma((24,)),
-            dma((16, 2)),
+            dma((5, PIECES)),
+            dma((4, PIECES)),
+            dma((12 * PIECES,)),
+            dma((16, PIECES)),
         ],
         compiler_params=pltpu.CompilerParams(
-            collective_id=0, has_side_effects=True, vmem_limit_bytes=48 << 20
+            collective_id=0, has_side_effects=True, vmem_limit_bytes=63 << 20
         ),
         cost_estimate=pl.CostEstimate(flops=2 * tokens * feats * 4096, bytes_accessed=4 << 20, transcendentals=0),
     )(projected.transpose(1, 0, 2), short_w, residues.T, rates.T, skip.reshape(1, chans), w_out)

time: 74.2 us -> 70.8 us (0.954)
  the two profiles are of different devices: /device:TPU:56 before, /device:TPU:128 now
where the time goes in v1:
time: 70.8 us; the launch traced here: 70.6 us
  Pallas kernels  68.7 us (97%)
  local copies, waits for them, and re-layouts  1.87 us (3%)
    pallas_call x1, Pallas kernels, body(): pl.pallas_call(functools.partial(kernel, length), out_shape=jax.ShapeDtyp...  68.7 us
    unnamed x1, local copies, waits for them, and re-layouts  1.87 us

profile of v1, /device:TPU:128, one launch (start us, length us, event | category | flops | bytes accessed | tf_op | source)
XLA Modules:
  0.0 70.6 jit_solution(4623719050075784687)
XLA Ops:
  0.0 68.7 %shard_map.64 = bf16[512,512]{1,0:T(8,128)(2,1)} custom-call(bf16[3,512,256]{2,1,0:T(8,128)(2,1)} %bitcast.4, f32[3,3,256]{2,1,0:T(4,128)} %short_hbm.1, f32[16,256]{1,0:T(8,128)} %bitcast.5, f32[16,256]{1,0:T(8,128)} %bitcast.6, f32[1,256]{1,0:T(1,128)} %bitcast.7, bf16[128,512]{1,0:T(8,128)(2,1)} %w_hbm.1), custom_call_target="tpu_custom_call" | custom-call | flops 2147483648 | bytes 4194304 | tf_op jit(solution)/shard_map/pallas_call | solution.py:507
  68.7 1.9 %copy.8 = bf16[512,512]{1,0:T(8,128)(2,1)} copy(bf16[512,512]{1,0:T(8,128)(2,1)} %shard_map.64) | data formatting | bytes 1048576

commit v2 on v1

--- a/solution.py
+++ b/solution.py
@@ -244,20 +244,42 @@
     e_low, e_high = jnp.where(low, own_edges, other_edges), jnp.where(low, other_edges, own_edges)
     m0, m1 = edge_inner((e_low[4:6], e_low[6:8]), (e_high[0:2], e_high[2:4]))
     chip_total = decay(tokens) * t_low + t_high + scale * (decay(tokens - 1) * m0 + decay(tokens - 2) * m1)
-    message = jnp.concatenate([chip_total, e_low[0:4], e_high[4:10], jnp.zeros((6, chans), F32)], axis=0)
-    msg[h] = message.astype(BF16)
-
-    def msg_copy(slot, step, chip):
+    for at, parts in enumerate(
+        (
+            (chip_total[0:8], e_low[0:4], jnp.zeros((4, chans), F32)),
+            (chip_total[8:16], e_high[4:10], jnp.zeros((2, chans), F32)),
+        )
+    ):
+        msg[h, at] = jnp.concatenate(parts, axis=0).astype(BF16)
+
+    def msg_copy(slot, part_at, step, seq):
         return pltpu.make_async_remote_copy(
-            src_ref=msg.at[slot], dst_ref=msg.at[slot], send_sem=msg_send.at[step], recv_sem=msg_recv.at[slot],
-            device_id=(chip * 2 + k, c), device_id_type=MESH,
+            src_ref=msg.at[slot, part_at], dst_ref=msg.at[slot, part_at], send_sem=msg_send.at[step],
+            recv_sem=msg_recv.at[slot, part_at], device_id=(seq, c), device_id_type=MESH,
         )
 
     def msg_go(step, _):
-        msg_copy(h, step, h + step).start()
+        msg_copy(h, k, step, (h + step) * 2 + k).start()
         return 0
 
     lax.fori_loop(1, 16 - h, msg_go, 0)
+
+    def w_chain(own, n):
+        zz, ups, downs = (zh, 4, 3) if own else (other_z, 3, 4)
+        if n == 0:
+            slot = seq_of(y, zz, k)
+            w_here(slot)
+            w_go(slot, seq_of(up_y, zh, k))
+            w_go(slot, seq_of(down_y, zh, k))
+            w_go(slot, partner)
+            return
+        for here, limit, onward in (((y + 8 - n) % 8, ups, up_y), ((y + n) % 8, downs, down_y)):
+            if n <= limit:
+                slot = seq_of(here, zz, k)
+                w_here(slot)
+                if n < limit:
+                    w_go(slot, seq_of(onward, zh, k))
+                w_go(slot, partner)
 
     loads[5].wait()
     other_z = 1 - zh
@@ -270,16 +292,25 @@
     far1, far2 = scale * decay(2 * tokens - 1), scale * decay(2 * tokens - 2)
 
     def put_edges(j):
-        values = msg[j, 16:32, :].astype(F32)
-        for tile in range(tiles):
-            edges[tile, pl.ds(j * 16 + 16, 16), :] = values[:, tile * LANES : tile * LANES + LANES]
+        for at in range(2):
+            values = msg[j, at].astype(F32)[8:16]
+            for tile in range(tiles):
+                edges[tile, pl.ds(j * 16 + 16 + 8 * at, 8), :] = values[:, tile * LANES : tile * LANES + LANES]
+
+    def half_here(j, _):
+        msg_copy(j, k, 0, s).wait_recv()
+        msg_copy(j, k, 16 + j, partner).start()
+        return 0
 
     def chip_here(j, _):
-        msg_copy(j, 0, h).wait_recv()
+        msg_copy(j, 1 - k, 0, s).wait_recv()
         put_edges(j)
         return 0
 
     put_edges(h)
+    w_chain(True, 1)
+    lax.fori_loop(0, h, half_here, 0)
+    w_chain(False, 0)
     lax.fori_loop(0, h, chip_here, 0)
     for tile in range(tiles):
         lanes = pl.ds(tile * LANES, LANES)
@@ -292,8 +323,8 @@
 
         (k0, k1), (v0, v1) = (
             (
-                w0 * edge_rows(2 * st, False) + w1 * edge_rows(5 + 2 * st, True) + w2 * edge_rows(4 + 2 * st, True),
-                w0 * edge_rows(2 * st + 1, False) + w1 * edge_rows(2 * st, False) + w2 * edge_rows(5 + 2 * st, True),
+                w0 * edge_rows(2 * st, False) + w1 * edge_rows(9 + 2 * st, True) + w2 * edge_rows(8 + 2 * st, True),
+                w0 * edge_rows(2 * st + 1, False) + w1 * edge_rows(2 * st, False) + w2 * edge_rows(9 + 2 * st, True),
             )
             for st, (w0, w1, w2) in enumerate((taps_of(1), taps_of(2)))
         )
@@ -303,12 +334,13 @@
     def add_chip(j, state):
         after = jnp.where(j == 0, 0.0, 1.0)
         u0, u1 = firsts[0, pl.ds(j, 1), :], firsts[1, pl.ds(j, 1), :]
-        return far * state + msg[j, 0:16, :].astype(F32) + after * (far1 * u0 + far2 * u1)
+        total = jnp.concatenate([msg[j, at].astype(F32)[0:8] for at in range(2)], axis=0)
+        return far * state + total + after * (far1 * u0 + far2 * u1)
 
     chip_in = lax.fori_loop(0, h, add_chip, jnp.zeros((MODES, chans), F32))
     f0, f1 = firsts[0, pl.ds(h, 1), :], firsts[1, pl.ds(h, 1), :]
     chip_first = jnp.where(h == 0, 0.0, 1.0)
-    chip_last_q = jnp.concatenate([edges[tile, pl.ds(h * 16 + 8, 2), :] for tile in range(tiles)], axis=1)
+    chip_last_q = jnp.concatenate([edges[tile, pl.ds(h * 16 + 12, 2), :] for tile in range(tiles)], axis=1)
     high_in = decay(tokens) * chip_in + t_low
     high_in += chip_first * scale * (decay(tokens - 1) * f0 + decay(tokens - 2) * f1)
     state_in = jnp.where(low, chip_in, high_in)
@@ -425,28 +457,13 @@
 
         lax.fori_loop(0, tokens // 256, block, 0)
 
-    def w_step(n):
-        if n == 1:
-            slot = seq_of(y, other_z, k)
-            w_here(slot)
-            w_go(slot, seq_of(up_y, zh, k))
-            w_go(slot, seq_of(down_y, zh, k))
-            w_go(slot, partner)
-        for zz, ups, downs in ((zh, 4, 3), (other_z, 3, 4)):
-            for here, limit, onward in (((y + 8 - n) % 8, ups, up_y), ((y + n) % 8, downs, down_y)):
-                if n <= limit:
-                    slot = seq_of(here, zz, k)
-                    w_here(slot)
-                    if n < limit:
-                        w_go(slot, seq_of(onward, zh, k))
-                    w_go(slot, partner)
-
     def w_other(at, _):
         w_here(at * 2 + 1 - k)
         return 0
 
     own_go()
-    w_step(1)
+    w_chain(True, 2)
+    w_chain(False, 1)
     along(1, 0)
     along(1, 1)
     pass_on(0, 0)
@@ -459,15 +476,17 @@
     along(1, 3)
     along(2, 2)
     along(2, 3)
-    w_step(2)
+    w_chain(True, 3)
+    w_chain(False, 2)
     for piece in range(PIECES):
         along(3, piece)
     for piece in (0, 2, 1, 3):
         pass_on(1, piece)
-    w_step(3)
+    w_chain(True, 4)
+    w_chain(False, 3)
     for piece in (0, 2, 1, 3):
         pass_on(2, piece)
-    w_step(4)
+    w_chain(False, 4)
     lax.fori_loop(0, 16, w_other, 0)
     everyone = tuple(place)
     multiply(0, everyone)
@@ -491,8 +510,14 @@
                 z_copy(c, piece, at, beside).wait_send()
 
     def msg_gone(step, _):
-        msg_copy(h, step, h).wait_send()
-        return 0
+        msg_copy(h, k, step, s).wait_send()
+        return 0
+
+    def half_gone(j, _):
+        msg_copy(j, k, 16 + j, partner).wait_send()
+        return 0
+
+    lax.fori_loop(0, h, half_gone, 0)
 
     lax.fori_loop(1, 16 - h, msg_gone, 0)
 
@@ -525,7 +550,7 @@
             pltpu.VMEM((MODES, SUBS, chans), F32),
             pltpu.VMEM((MODES, chans), F32),
             pltpu.VMEM((2, 32, chans), BF16),
-            pltpu.VMEM((16, 32, chans), BF16),
+            pltpu.VMEM((16, 2, 16, chans), BF16),
             pltpu.VMEM((tiles, 17 * 16, LANES), F32),
             pltpu.VMEM((2, 16, chans), F32),
             pltpu.VMEM((tiles, tokens, LANES), F32),
@@ -534,8 +559,8 @@
             pltpu.VMEM((tokens, feats), F32),
             dma((6,)),
             dma((2,)),
-            dma((16,)),
-            dma((16,)),
+            dma((32,)),
+            dma((16, 2)),
             dma((32,)),
             dma((32,)),
             dma((5, PIECES)),

time: 70.8 us -> 69.9 us (0.987)
  the two profiles are of different devices: /device:TPU:128 before, /device:TPU:56 now
where the time goes in v2:
time: 69.9 us; the launch traced here: 69.7 us
  Pallas kernels  67.9 us (97%)
  local copies, waits for them, and re-layouts  1.87 us (3%)
    pallas_call x1, Pallas kernels, body(): pl.pallas_call(functools.partial(kernel, length), out_shape=jax.ShapeDtyp...  67.9 us
    unnamed x1, local copies, waits for them, and re-layouts  1.87 us

profile of v2, /device:TPU:56, one launch (start us, length us, event | category | flops | bytes accessed | tf_op | source)
XLA Modules:
  0.0 69.7 jit_solution(15485292968179216224)
XLA Ops:
  0.0 67.9 %shard_map.64 = bf16[512,512]{1,0:T(8,128)(2,1)} custom-call(bf16[3,512,256]{2,1,0:T(8,128)(2,1)} %bitcast.4, f32[3,3,256]{2,1,0:T(4,128)} %short_hbm.1, f32[16,256]{1,0:T(8,128)} %bitcast.5, f32[16,256]{1,0:T(8,128)} %bitcast.6, f32[1,256]{1,0:T(1,128)} %bitcast.7, bf16[128,512]{1,0:T(8,128)(2,1)} %w_hbm.1), custom_call_target="tpu_custom_call" | custom-call | flops 2147483648 | bytes 4194304 | tf_op jit(solution)/shard_map/pallas_call | solution.py:532
  67.9 1.9 %copy.8 = bf16[512,512]{1,0:T(8,128)(2,1)} copy(bf16[512,512]{1,0:T(8,128)(2,1)} %shard_map.64) | data formatting | bytes 1048576

commit v3 on v2

--- a/solution.py
+++ b/solution.py
@@ -57,6 +57,7 @@
     g_all,
     w_all,
     acc,
+    result,
     load_sem,
     pair_sem,
     msg_send,
@@ -76,7 +77,7 @@
     tokens, chans = proj.shape[1], proj.shape[2]
     tiles = chans // LANES
     steps = tokens // SUBS
-    rows_of_piece = tokens // PIECES
+    half = tokens // 2
 
     def seq_of(yy, zz, kk):
         return yy * 4 + zz * 2 + kk
@@ -349,6 +350,58 @@
     q_last = jnp.where(low, chip_last_q, e_low[8:10])
     q_first = edge((q_last,), (ends(0, True),), (0,))[0]
 
+    end = (zl == 0) | (zl == 3)
+    beside = x * 4 + zl + 1 - 2 * (zl % 2)
+    middle = x * 4 + 3 - zl
+    order = (zl, zl + 1 - 2 * (zl % 2), 2 - zl // 2, 3 - 3 * (zl // 2))
+
+    def z_copy(slot, piece, at, chan):
+        ref = g_all.at[slot, piece // 2, pl.ds(piece % 2 * half, half)]
+        return pltpu.make_async_remote_copy(
+            src_ref=ref, dst_ref=ref, send_sem=z_send.at[at, piece],
+            recv_sem=z_recv.at[slot % 4, piece], device_id=(s, chan), device_id_type=MESH,
+        )
+
+    def x_copy(slot, piece, at, xx):
+        ref = g_all.at[slot, piece // 2, pl.ds(piece % 2 * half, half)]
+        return pltpu.make_async_remote_copy(
+            src_ref=ref, dst_ref=ref, send_sem=x_send.at[at],
+            recv_sem=x_recv.at[slot, piece], device_id=(s, xx * 4 + zl), device_id_type=MESH,
+        )
+
+    x_started = []
+
+    def x_go(slot, piece, xx):
+        copy = x_copy(slot, piece, len(x_started), xx)
+        copy.start()
+        x_started.append(copy)
+
+    def x_here(slot, piece):
+        x_copy(slot, piece, 0, right).wait_recv()
+
+    def own_go(tile):
+        for piece, other in ((2 * tile, 2 * tile + 1), (2 * tile + 1, 2 * tile)):
+            z_copy(c, piece, 0, beside).start()
+            x_go(c, piece, right)
+            pl.when(jnp.logical_not(end))(lambda piece=piece: z_copy(c, piece, 1, middle).start())
+            x_go(c, other, left)
+
+    def along(i, piece):
+        slot = x * 4 + order[i]
+        z_copy(slot, piece, 0, beside).wait_recv()
+        onward = middle if i == 1 else beside
+        pl.when(jnp.logical_not(end))(lambda: z_copy(slot, piece, 1 + i, onward).start())
+        x_go(slot, piece, right)
+        x_go(slot, piece, left)
+
+    def pass_on(i, piece):
+        if piece % 2 == 0:
+            slot, onward = left * 4 + order[i], right
+        else:
+            slot, onward = right * 4 + order[i], left
+        x_here(slot, piece)
+        x_go(slot, piece, onward)
+
     for tile in range(tiles):
         cut = slice(tile * LANES, tile * LANES + LANES)
         lanes = pl.ds(tile * LANES, LANES)
@@ -379,97 +432,52 @@
         state = gate_step(0, state, 0)
         state = gate_step(1, state, 1)
         lax.fori_loop(2, steps, gate_step, state)
-    for tile in range(tiles):
-        g_all[c, :, pl.ds(tile * LANES, LANES)] = g_wide[tile].astype(BF16)
-
-    end = (zl == 0) | (zl == 3)
-    beside = x * 4 + zl + 1 - 2 * (zl % 2)
-    middle = x * 4 + 3 - zl
-    order = (zl, zl + 1 - 2 * (zl % 2), 2 - zl // 2, 3 - 3 * (zl // 2))
-
-    def z_copy(slot, piece, at, chan):
-        rows = pl.ds(piece * rows_of_piece, rows_of_piece)
-        return pltpu.make_async_remote_copy(
-            src_ref=g_all.at[slot, rows], dst_ref=g_all.at[slot, rows], send_sem=z_send.at[at, piece],
-            recv_sem=z_recv.at[slot % 4, piece], device_id=(s, chan), device_id_type=MESH,
-        )
-
-    def x_copy(slot, piece, at, xx):
-        rows = pl.ds(piece * rows_of_piece, rows_of_piece)
-        return pltpu.make_async_remote_copy(
-            src_ref=g_all.at[slot, rows], dst_ref=g_all.at[slot, rows], send_sem=x_send.at[at],
-            recv_sem=x_recv.at[slot, piece], device_id=(s, xx * 4 + zl), device_id_type=MESH,
-        )
-
-    x_started = []
-
-    def x_go(slot, piece, xx):
-        copy = x_copy(slot, piece, len(x_started), xx)
-        copy.start()
-        x_started.append(copy)
-
-    def x_here(slot, piece):
-        x_copy(slot, piece, 0, right).wait_recv()
-
-    def own_go():
-        for piece in range(PIECES):
-            z_copy(c, piece, 0, beside).start()
-            x_go(c, piece, right)
-            pl.when(jnp.logical_not(end))(lambda piece=piece: z_copy(c, piece, 1, middle).start())
-            x_go(c, (piece + PIECES // 2) % PIECES, left)
-
-    def along(i, piece):
-        slot = x * 4 + order[i]
-        z_copy(slot, piece, 0, beside).wait_recv()
-        onward = middle if i == 1 else beside
-        pl.when(jnp.logical_not(end))(lambda: z_copy(slot, piece, 1 + i, onward).start())
-        x_go(slot, piece, right)
-        x_go(slot, piece, left)
-
-    def pass_on(i, piece):
-        if piece < PIECES // 2:
-            slot, onward = left * 4 + order[i], right
-        else:
-            slot, onward = right * 4 + order[i], left
-        x_here(slot, piece)
-        x_go(slot, piece, onward)
+        g_all[c, tile] = g_wide[tile].astype(BF16)
+        own_go(tile)
 
     place = dict(own=x, left=left, right=right, across=across)
 
-    def multiply(i, sides):
-        for piece in range(PIECES):
-            if 'left' in sides and piece >= PIECES // 2:
+    def arrived(i, sides, odd):
+        for piece in (odd, 2 + odd):
+            if 'left' in sides and odd:
                 x_here(left * 4 + order[i], piece)
-            if 'right' in sides and piece < PIECES // 2:
+            if 'right' in sides and not odd:
                 x_here(right * 4 + order[i], piece)
             if 'across' in sides:
                 x_here(across * 4 + order[i], piece)
 
+    def products(i, sides, at):
+        value = acc[at]
+        for side in sides:
+            slot = place[side] * 4 + order[i]
+            rows = w_all[pl.ds(2 * slot, 2)].reshape(chans, -1)
+            left_side = jnp.concatenate([g_all[slot, tile, at] for tile in range(tiles)], axis=1)
+            value = value + jnp.dot(left_side, rows, preferred_element_type=F32)
+        return value
+
+    def multiply(i, sides):
+        for odd in range(2):
+            arrived(i, sides, odd)
+
         def block(at, _):
-            at = pl.ds(pl.multiple_of(at * 256, 256), 256)
-            value = acc[at]
-            for side in sides:
-                slot = place[side] * 4 + order[i]
-                rows = w_all[pl.ds(2 * slot, 2)].reshape(chans, -1)
-                value = value + jnp.dot(g_all[slot, at], rows, preferred_element_type=F32)
-            acc[at] = value
+            at = pl.ds(pl.multiple_of(at * half, half), half)
+            acc[at] = products(i, sides, at)
             return 0
 
-        lax.fori_loop(0, tokens // 256, block, 0)
+        lax.fori_loop(0, 2, block, 0)
 
     def w_other(at, _):
         w_here(at * 2 + 1 - k)
         return 0
 
-    own_go()
     w_chain(True, 2)
     w_chain(False, 1)
     along(1, 0)
     along(1, 1)
     pass_on(0, 0)
+    pass_on(0, 1)
+    along(2, 0)
     pass_on(0, 2)
-    along(2, 0)
-    pass_on(0, 1)
     pass_on(0, 3)
     along(1, 2)
     along(2, 1)
@@ -480,23 +488,28 @@
     w_chain(False, 2)
     for piece in range(PIECES):
         along(3, piece)
-    for piece in (0, 2, 1, 3):
+    for piece in range(PIECES):
         pass_on(1, piece)
     w_chain(True, 4)
     w_chain(False, 3)
-    for piece in (0, 2, 1, 3):
+    for piece in range(PIECES):
         pass_on(2, piece)
     w_chain(False, 4)
     lax.fori_loop(0, 16, w_other, 0)
     everyone = tuple(place)
     multiply(0, everyone)
     multiply(1, everyone)
-    for piece in (0, 2, 1, 3):
+    for piece in range(PIECES):
         pass_on(3, piece)
     multiply(2, everyone)
     multiply(3, ('own', 'left', 'right'))
-    multiply(3, ('across',))
-    out[...] = acc[...].astype(BF16)
+    out_copies = []
+    for odd in range(2):
+        at = pl.ds(odd * half, half)
+        arrived(3, ('across',), odd)
+        result[at] = products(3, ('across',), at).astype(BF16)
+        out_copies.append(pltpu.make_async_copy(result.at[at], out.at[at], load_sem.at[odd]))
+        out_copies[-1].start()
 
     for copy in x_started + w_started:
         copy.wait_send()
@@ -520,6 +533,8 @@
     lax.fori_loop(0, h, half_gone, 0)
 
     lax.fori_loop(1, 16 - h, msg_gone, 0)
+    for copy in out_copies:
+        copy.wait()
 
 
 def body(projected, short_w, residues, rates, skip, w_out):
@@ -527,13 +542,12 @@
     rows, feats = w_out.shape
     length = tokens * lax.axis_size("seq")
     tiles, steps = chans // LANES, tokens // SUBS
-    vmem = pl.BlockSpec(memory_space=pltpu.VMEM)
     dma = pltpu.SemaphoreType.DMA
     return pl.pallas_call(
         functools.partial(kernel, length),
         out_shape=jax.ShapeDtypeStruct((tokens, feats), BF16),
         in_specs=[pl.BlockSpec(memory_space=pltpu.HBM)] * 6,
-        out_specs=vmem,
+        out_specs=pl.BlockSpec(memory_space=pltpu.HBM),
         scratch_shapes=[
             pltpu.VMEM((3, tokens, chans), BF16),
             pltpu.VMEM((3, 3, chans), F32),
@@ -554,9 +568,10 @@
             pltpu.VMEM((tiles, 17 * 16, LANES), F32),
             pltpu.VMEM((2, 16, chans), F32),
             pltpu.VMEM((tiles, tokens, LANES), F32),
-            pltpu.VMEM((16, tokens, chans), BF16),
+            pltpu.VMEM((16, tiles, tokens, LANES), BF16),
             pltpu.VMEM((32, rows, feats), BF16),
             pltpu.VMEM((tokens, feats), F32),
+            pltpu.VMEM((tokens, feats), BF16),
             dma((6,)),
             dma((2,)),
             dma((32,)),

time: 69.9 us -> 68.5 us (0.980)
  Pallas kernels: 67.9 us -> 66.5 us
    pallas_call x1, Pallas kernels: 67.9 us -> 66.5 us  [body(): pl.pallas_call(functools.partial(kernel, length), out_shape=jax.ShapeDtyp...]
where the time goes in v3:
time: 68.5 us; the launch traced here: 68.4 us
  Pallas kernels  66.5 us (97%)
  local copies, waits for them, and re-layouts  1.87 us (3%)
    pallas_call x1, Pallas kernels, body(): pl.pallas_call(functools.partial(kernel, length), out_shape=jax.ShapeDtyp...  66.5 us
    unnamed x1, local copies, waits for them, and re-layouts  1.87 us

profile of v3, /device:TPU:56, one launch (start us, length us, event | category | flops | bytes accessed | tf_op | source)
XLA Modules:
  0.0 68.4 jit_solution(8466883648759409415)
XLA Ops:
  0.0 66.5 %shard_map.64 = bf16[512,512]{1,0:T(8,128)(2,1)} custom-call(bf16[3,512,256]{2,1,0:T(8,128)(2,1)} %bitcast.4, f32[3,3,256]{2,1,0:T(4,128)} %short_hbm.1, f32[16,256]{1,0:T(8,128)} %bitcast.5, f32[16,256]{1,0:T(8,128)} %bitcast.6, f32[1,256]{1,0:T(1,128)} %bitcast.7, bf16[128,512]{1,0:T(8,128)(2,1)} %w_hbm.1), custom_call_target="tpu_custom_call" | custom-call | flops 2147483648 | bytes 4194304 | tf_op jit(solution)/shard_map/pallas_call | solution.py:546
  66.5 1.9 %copy.8 = bf16[512,512]{1,0:T(8,128)(2,1)} copy(bf16[512,512]{1,0:T(8,128)(2,1)} %shard_map.64) | data formatting | bytes 1048576

commit v4 on v3

--- a/solution.py
+++ b/solution.py
@@ -503,11 +503,18 @@
         pass_on(3, piece)
     multiply(2, everyone)
     multiply(3, ('own', 'left', 'right'))
+    far_slot = across * 4 + order[3]
+    far_rows = w_all.at[pl.ds(2 * far_slot, 2)]
+    for odd in range(2):
+        at = pl.ds(odd * half, half)
+        x_here(far_slot, odd)
+        acc[at] += jnp.dot(g_all[far_slot, 0, at], far_rows[0], preferred_element_type=F32)
     out_copies = []
     for odd in range(2):
         at = pl.ds(odd * half, half)
-        arrived(3, ('across',), odd)
-        result[at] = products(3, ('across',), at).astype(BF16)
+        x_here(far_slot, 2 + odd)
+        last = jnp.dot(g_all[far_slot, 1, at], far_rows[1], preferred_element_type=F32)
+        result[at] = (acc[at] + last).astype(BF16)
         out_copies.append(pltpu.make_async_copy(result.at[at], out.at[at], load_sem.at[odd]))
         out_copies[-1].start()
 

time: 68.5 us -> 68.5 us (level)
  no operation moved by 1% of the time
where the time goes in v4:
time: 68.5 us; the launch traced here: 68.3 us
  Pallas kernels  66.4 us (97%)
  local copies, waits for them, and re-layouts  1.87 us (3%)
    pallas_call x1, Pallas kernels, body(): pl.pallas_call(functools.partial(kernel, length), out_shape=jax.ShapeDtyp...  66.4 us
    unnamed x1, local copies, waits for them, and re-layouts  1.87 us

profile of v4, /device:TPU:56, one launch (start us, length us, event | category | flops | bytes accessed | tf_op | source)
XLA Modules:
  0.0 68.3 jit_solution(12347854137505533200)
XLA Ops:
  0.0 66.4 %shard_map.64 = bf16[512,512]{1,0:T(8,128)(2,1)} custom-call(bf16[3,512,256]{2,1,0:T(8,128)(2,1)} %bitcast.4, f32[3,3,256]{2,1,0:T(4,128)} %short_hbm.1, f32[16,256]{1,0:T(8,128)} %bitcast.5, f32[16,256]{1,0:T(8,128)} %bitcast.6, f32[1,256]{1,0:T(1,128)} %bitcast.7, bf16[128,512]{1,0:T(8,128)(2,1)} %w_hbm.1), custom_call_target="tpu_custom_call" | custom-call | flops 2147483648 | bytes 4194304 | tf_op jit(solution)/shard_map/pallas_call | solution.py:553
  66.4 1.9 %copy.8 = bf16[512,512]{1,0:T(8,128)(2,1)} copy(bf16[512,512]{1,0:T(8,128)(2,1)} %shard_map.64) | data formatting | bytes 1048576
